TPU v7x, 32 devices: a whole 2x2x4 slice. The times are simulated.
32 devices in a mesh: wide: 16 (over z, y, core), narrow: 2 (over x).
Axes of the slice: x: 2, y: 2, z: 4, core: 2. Of those that a mesh axis runs over, the one named last changes fastest.
Arguments:
- embedded_patches: bfloat16 [4096, 1280], P(('wide', 'narrow')), may hold values from -6 to 6
- sequence_number: int32 [4096], P(('wide', 'narrow')), may hold values from 0 to 1023, never falling along the last dimension, each value on 1 to 16 neighbouring positions
- filler_flag: int32 [4096], P(('wide', 'narrow')), may hold values 0 or 1
- triple_projection_matrix: bfloat16 [2, 1280, 3840], P(None, ('wide', 'narrow')), may hold values from -0.15625 to 0.15625
- mixing_exit_matrix: bfloat16 [2, 1280, 1280], P(None, ('wide', 'narrow')), may hold values from -0.3125 to 0.3125
- perceptron_expand_matrix: bfloat16 [2, 1280, 5120], P(None, ('wide', 'narrow')), may hold values from -0.15625 to 0.15625
- perceptron_shrink_matrix: bfloat16 [2, 5120, 1280], P(None, ('wide', 'narrow')), may hold values from -0.078125 to 0.078125
- premix_scale_vector: bfloat16 [2, 1280], P(None, ('wide', 'narrow')), may hold values from 0.5 to 1.5
- preperceptron_scale_vector: bfloat16 [2, 1280], P(None, ('wide', 'narrow')), may hold values from 0.5 to 1.5
- readout_first_matrix: bfloat16 [1280, 1280], replicated, may hold values from -0.15625 to 0.15625
- readout_first_offset: bfloat16 [1280], replicated, may hold values from -3 to 3
- readout_final_matrix: bfloat16 [1280, 1280], P(None, 'narrow'), may hold values from -0.15625 to 0.15625
- prediction_offset: bfloat16 [1280], P('narrow'), may hold values from -3 to 3
- readout_shortcut_matrix: bfloat16 [1280, 1280], P(None, 'narrow'), may hold values from -0.15625 to 0.15625
- prediction_adjoint: bfloat16 [4096, 1280], P('wide', 'narrow'), may hold values from -6 to 6
Outputs:
- predictions: bfloat16 [4096, 1280], P('wide', 'narrow')
- input_grad: float32 [4096, 1280], P(('wide', 'narrow'))
- qkv_grad: float32 [2, 1280, 3840], P(None, ('wide', 'narrow'))
- out_grad: float32 [2, 1280, 1280], P(None, ('wide', 'narrow'))
- in_grad: float32 [2, 1280, 5120], P(None, ('wide', 'narrow'))
- down_grad: float32 [2, 5120, 1280], P(None, ('wide', 'narrow'))
- attn_gain_grad: float32 [2, 1280], P(None, ('wide', 'narrow'))
- mlp_gain_grad: float32 [2, 1280], P(None, ('wide', 'narrow'))
- head_in_grad: float32 [1280, 1280], P(('wide', 'narrow'))
- head_in_bias_grad: float32 [1280], P(('wide', 'narrow'))
- head_out_grad: float32 [1280, 1280], P('wide', 'narrow')
- head_out_bias_grad: float32 [1280], P('narrow')
- head_skip_grad: float32 [1280, 1280], P('wide', 'narrow')
Inputs may be any that keep to these rules, and one draw needn't show every extreme that they name: `sequence_number`: segment numbers never fall along the tokens, and one segment spans 1 to 16 tokens.
All inputs are finite; a program needn't handle non-finite values. No bound on the sum of `filler_flag` on one device may be relied on, other than what follows from the above.
Results may differ from a plain program's by a relative error of at most 0.019.
Values may be sent and summed in bfloat16 or wider, within the bound.
A program may use at most 640 MiB of HBM per device.

v0:
```python
import math

import jax
import jax.numpy as jnp
import numpy as np
from jax import lax
from jax.experimental import pallas as pl
from jax.experimental.pallas import tpu as pltpu
from jax.sharding import PartitionSpec as P

HDIM = 80
HALF = HDIM // 2
LAYERS = 2
ROW_LEN = 16
BLOCK = 128
HALF_BLOCK = BLOCK // 2
PLANE = 8
PHASES = 2 * LAYERS
MESH = pl.DeviceIdType.MESH
BF = jnp.bfloat16
F32 = jnp.float32
EPS = 1e-06
ROTARY_BASE = 10000.0
MIB = 1024 * 1024
VMEM = pl.BlockSpec(memory_space=pltpu.VMEM)
ANY = pl.BlockSpec(memory_space=pl.ANY)


def up16(rows):
    return -(-rows // 16) * 16


def rows_at(start, count, step=16):
    return pl.ds(pl.multiple_of(start, step), count)


def dot(a, b, ca=1, cb=0):
    return lax.dot_general(a, b, (((ca,), (cb,)), ((), ())), preferred_element_type=F32)


class Place:
    def __init__(self):
        wide = lax.axis_index("wide")
        self.x = lax.axis_index("narrow")
        self.core = wide % 2
        self.y = (wide // 2) % 2
        self.z = wide // 4

    def device(self, z, y, core, x):
        return (z * 4 + y * 2 + core, x)

    def sibling(self):
        return self.device(self.z, self.y, 1 - self.core, self.x)

    def major(self, s, far=0):
        return (self.y + s * (self.x - self.y) + far) % 2

    def minor(self, s, near=0):
        return (self.x + s * (self.y - self.x) + near) % 2

    def near(self, s):
        return self.device(self.z, (self.y + s) % 2, self.core, (self.x + 1 - s) % 2)

    def far(self, s):
        return self.device(self.z, (self.y + 1 - s) % 2, self.core, (self.x + s) % 2)

    def level(self, z):
        return self.device(z, self.y, self.core, self.x)

    def turned(self, e):
        return (self.y + e // 4) % 2, (self.core + e // 2) % 2, (self.x + e) % 2

    def other(self, e):
        return self.device(self.z, *self.turned(e))

    def rank(self, e=0):
        y, core, x = self.turned(e)
        return 4 * y + 2 * core + x

    def indexed(self, index):
        return (index // 2, index % 2)

    def holder(self, levels):
        index = PLANE * self.z + self.rank()
        return index % levels * PLANE + index // levels

    def held(self, levels):
        return levels * self.rank() + self.z

    def trades(self, levels):
        return self.holder(levels) != PLANE * self.z + self.rank()


def greet(place, levels):
    barrier = pltpu.get_barrier_semaphore()
    others = [place.other(e) for e in range(1, PLANE)]
    others += [place.level((place.z + d) % levels) for d in range(1, levels)]
    for other in others:
        pl.semaphore_signal(barrier, inc=1, device_id=other, device_id_type=MESH)
    trades = place.trades(levels)

    @pl.when(trades)
    def _():
        for index in (place.holder(levels), place.held(levels)):
            pl.semaphore_signal(
                barrier, inc=1, device_id=place.indexed(index), device_id_type=MESH
            )
        pl.semaphore_wait(barrier, len(others) + 2)

    @pl.when(jnp.logical_not(trades))
    def _():
        pl.semaphore_wait(barrier, len(others))


def remote(src, dst, send, recv, device):
    return pltpu.make_async_remote_copy(
        src_ref=src, dst_ref=dst, send_sem=send, recv_sem=recv, device_id=device,
        device_id_type=MESH,
    )


class Exchange:
    def __init__(self, place, phase, buf, scratch):
        (self.part, self.recv_s, self.send_f, self.recv_f, self.send_n, self.recv_n, self.sems) = scratch
        self.place, self.phase, self.buf = place, phase, buf

    def copy(self, s, kind, src, dst, device):
        sems = self.sems
        return remote(
            src, dst, sems.at[self.phase, s, 0, kind], sems.at[self.phase, s, 1, kind], device
        )

    def block(self, s, far, near, core):
        place = self.place
        return self.buf.at[s, place.major(s, far), place.minor(s, near), core]

    def own(self, s):
        return (s, self.place.major(s), self.place.minor(s), self.place.core)

    def to_near(self, s, far=0, near=0):
        rows = self.block(s, far, near, self.place.core)
        return self.copy(s, 0, rows, rows, self.place.near(s))

    def to_far(self, s, far=0, near=0):
        rows = self.block(s, far, near, self.place.core)
        return self.copy(s, 1, rows, rows, self.place.far(s))

    def pass_far(self, s, far=0, near=1):
        rows = self.block(s, far, near, self.place.core)
        return self.copy(s, 2, rows, rows, self.place.far(s))

    def sibling(self, s, kind, core):
        if kind < 2:
            rows = self.block(s, 0, kind, core)
        else:
            rows = self.buf.at[s, self.place.major(s, 1), :, core]
        return self.copy(s, 3 + kind, rows, rows, self.place.sibling())

    def to_sibling(self, s, kind):
        return self.sibling(s, kind, self.place.core)

    def from_sibling(self, s, kind):
        return self.sibling(s, kind, 1 - self.place.core)

    def sum_sibling(self, s, half):
        src = self.part.at[s, half, :, 1 - self.place.core]
        sems = self.sems
        return remote(
            src, self.recv_s.at[s, half], sems.at[self.phase, s, 0, 6 + half],
            sems.at[self.phase, s, 1, 6 + half], self.place.sibling(),
        )

    def sum_far(self, s):
        return self.copy(s, 8, self.send_f.at[s], self.recv_f.at[s], self.place.far(s))

    def sum_near(self, s):
        return self.copy(s, 9, self.send_n.at[s], self.recv_n.at[s], self.place.near(s))

    def start(self, s):
        self.to_near(s).start()
        self.to_far(s).start()
        self.to_sibling(s, 0).start()

    def far_stage(self, s):
        self.sum_sibling(s, 1).wait_recv()
        own = self.part[s, 1, :, self.place.core].astype(F32)
        self.send_f[s] = (own + self.recv_s[s, 1].astype(F32)).astype(BF)
        self.sum_far(s).start()

    def summed(self, s, minor):
        own = self.part[s, 0, minor, self.place.core].astype(F32)
        return own + self.recv_s[s, 0, minor].astype(F32) + self.recv_f[s, minor].astype(F32)

    def near_stage(self, s):
        self.sum_sibling(s, 0).wait_recv()
        self.sum_far(s).wait_recv()
        self.send_n[s] = self.summed(s, self.place.minor(s, 1)).astype(BF)
        self.sum_near(s).start()

    def total(self, s):
        self.sum_near(s).wait_recv()
        total = self.summed(s, self.place.minor(s)) + self.recv_n[s].astype(F32)
        self.to_near(s).wait_send()
        self.to_far(s).wait_send()
        self.pass_far(s).wait_send()
        for kind in range(3):
            self.to_sibling(s, kind).wait_send()
        for half in range(2):
            self.sum_sibling(s, half).wait_send()
        self.sum_far(s).wait_send()
        self.sum_near(s).wait_send()
        return total

    def take_near(self, s):
        self.to_near(s, 0, 1).wait_recv()
        self.pass_far(s).start()
        self.to_sibling(s, 1).start()

    def take_far(self, s):
        self.to_far(s, 1, 0).wait_recv()
        self.pass_far(s, 1, 1).wait_recv()
        self.to_sibling(s, 2).start()

    def take_sibling(self, s):
        for kind in range(3):
            self.from_sibling(s, kind).wait_recv()

    def run(self, compute, hooks, taken=False):
        def body(i, carry):
            s, half = i // 2, i % 2
            if not taken:
                pl.when(half == 0)(lambda: self.take_near(s))

            for at, hook in hooks:
                pl.when(i == at)(hook)

            if not taken:
                @pl.when(half == 0)
                def _():
                    self.from_sibling(s, 0).wait_recv()
                    self.from_sibling(s, 1).wait_recv()

                pl.when(half == 1)(lambda: self.take_far(s))

            @pl.when(i == 2)
            def _():
                self.far_stage(0)

            if not taken:
                pl.when(half == 1)(lambda: self.from_sibling(s, 2).wait_recv())

            major = self.place.major(s, half)
            compute(s * 8 * HALF_BLOCK + major * 4 * HALF_BLOCK, s, half, major)
            self.sum_sibling(s, half).start()
            return carry

        lax.fori_loop(0, 4, body, 0)
        self.near_stage(0)
        self.far_stage(1)


def exchange_scratch(width, phases):
    return [
        pltpu.VMEM((2, 2, 2, 2, HALF_BLOCK, width), BF),
        pltpu.VMEM((2, 2, 2, HALF_BLOCK, width), BF),
        pltpu.VMEM((2, 2, HALF_BLOCK, width), BF),
        pltpu.VMEM((2, 2, HALF_BLOCK, width), BF),
        pltpu.VMEM((2, HALF_BLOCK, width), BF),
        pltpu.VMEM((2, HALF_BLOCK, width), BF),
        pltpu.SemaphoreType.DMA((phases, 2, 2, 10)),
    ]


def flat(ref, columns=slice(None)):
    if len(ref.shape) == 2:
        return ref[:, columns]
    values = ref[(slice(None),) * 5 + (columns,)]
    return values.reshape(-1, values.shape[-1])


def write_part(part, s, half, values, w, contracted):
    width = part.shape[-1]
    step = width // 2
    for n in range(0, width, step):
        columns = slice(n, n + step)
        side = w[:, columns] if contracted == 0 else w[columns, :]
        part[s, half, :, :, :, columns] = blocked(dot(values, side, 1, contracted).astype(BF))


def blocked(values):
    return values.reshape(2, 2, HALF_BLOCK, values.shape[-1])


def root(values):
    return lax.rsqrt(jnp.mean(values * values, axis=-1, keepdims=True) + EPS)


def forward_kernel(levels, *refs):
    (x_in, own_mask, rope, sel_q, sel_o, head_lanes, adjoint, bias_first, bias_last) = refs[:9]
    (gains, w_q, w_in, w_out) = refs[9:13]
    w_down, head_weights = refs[13], refs[14:17]
    (predictions, grad_out, xs, mid) = refs[17:21]
    kept, (slab_q, slab_o, slab_i, slab_d) = refs[21:33], refs[33:37]
    exchange = refs[37:44]
    (nrm, nml, qkv, prb, att, gl, act) = refs[44:51]
    slabs = refs[51:55]
    (wide_q, first, final, pick, first_q, final_q) = refs[55:61]
    (g, g_rows, hidden, gpre, picked, hidden_all) = refs[61:67]
    (mask, cut, pasted, o_cut, o_piece) = refs[67:72]
    (z_sems, own_sems, keep_sems, load_sems, g_sems, trade_sems, mask_sems, o_sems) = refs[72:]
    slab_outs = (slab_q, slab_o, slab_i, slab_d)
    place = Place()
    z = place.z
    heads = sel_o.shape[1] // BLOCK
    lanes = heads * BLOCK
    kept_here, waited = [], []

    def keep(src, dst):
        copy = pltpu.make_async_copy(src, dst, keep_sems.at[len(kept_here)])
        copy.start()
        kept_here.append(copy)
        return copy

    def forget(copy):
        copy.wait()
        waited.append(copy)

    relayed = levels == 4

    def far(delta):
        there = (z + delta) % levels
        return (z + there == 3) & (z * there == 0)

    counts = [slabs[0].shape[1] // levels, o_piece.shape[1], slabs[2].shape[1] // levels,
              w_down.shape[1]]

    def rows_of(m, level):
        return rows_at(level * counts[m], counts[m])

    def piece(layer, m):
        if m == 1:
            return o_piece.at[layer]
        if m == 3:
            return w_down.at[layer]
        return slabs[m].at[layer, rows_of(m, z)]

    def spread(layer, m, delta):
        return remote(
            piece(layer, m), slabs[m].at[layer, rows_of(m, z)],
            z_sems.at[0, layer, m, delta - 1], z_sems.at[1, layer, m, delta - 1],
            place.level((z + delta) % levels),
        )

    def arriving(layer, m, delta):
        rows = slabs[m].at[layer, rows_of(m, (z + levels - delta) % levels)]
        return remote(
            rows, rows, z_sems.at[0, layer, m, delta - 1], z_sems.at[1, layer, m, delta - 1],
            place.level((z + delta) % levels),
        )

    def relay(layer, m):
        rows = slabs[m].at[layer, rows_of(m, (z + 2) % levels)]
        return remote(
            rows, rows, z_sems.at[2, layer, m, 0], z_sems.at[1, layer, m, 2 * (z - 1)],
            place.level(3 * (z - 1)),
        )

    def for_spread(layer, m, act_on):
        for delta in range(1, levels):
            if relayed and delta != 2:
                @pl.when(jnp.logical_not(far(delta)))
                def _(delta=delta):
                    act_on(spread(layer, m, delta))
            else:
                act_on(spread(layer, m, delta))

    def own_piece(layer, m):
        return pltpu.make_async_copy(
            piece(layer, m), slabs[m].at[layer, rows_of(m, z)], own_sems.at[layer, m]
        )

    def send_weights(layer, m):
        if m % 2:
            own_piece(layer, m).start()
        for_spread(layer, m, lambda copy: copy.start())

    rows, q_cols = w_q.shape[1], slabs[0].shape[2]
    span = w_q.shape[2] // 3 // PLANE
    ff_rows = w_in.shape[2] // PLANE // levels
    padded = slabs[2].shape[2] // levels - ff_rows

    def cut_weights(layer):
        scaled_q = w_q[layer].astype(F32) * gains[0, layer]
        scaled_i = w_in[layer].astype(F32) * gains[1, layer]
        for t in range(PLANE):
            parts = []
            for kind in range(3):
                low = (kind * PLANE + t) * span
                parts.append(scaled_q[:, low : low + span])
            if q_cols > 3 * span:
                parts.append(jnp.zeros((rows, q_cols - 3 * span), F32))
            cut[layer, t, :rows, :q_cols] = jnp.concatenate(parts, axis=1).astype(BF)
            parts = []
            for zz in range(levels):
                low = (zz * PLANE + t) * ff_rows
                parts.append(scaled_i[:, low : low + ff_rows])
                if padded:
                    parts.append(jnp.zeros((rows, padded), F32))
            cut[layer, t, :rows, q_cols:] = jnp.concatenate(parts, axis=1).astype(BF)

    def trade(layer, e):
        return remote(
            cut.at[layer, place.rank(e)], pasted.at[layer, place.rank()],
            trade_sems.at[0, layer, e], trade_sems.at[1, layer, e], place.other(e),
        )

    def traded(layer, e):
        there = pasted.at[layer, place.rank(e)]
        return remote(
            there, there, trade_sems.at[0, layer, e], trade_sems.at[1, layer, e], place.other(e)
        )

    def start_trade(layer):
        for e in range(1, PLANE):
            trade(layer, e).start()
        own = place.rank()
        pltpu.make_async_copy(
            cut.at[layer, own], pasted.at[layer, own], trade_sems.at[0, layer, 0]
        ).start()

    def end_trade(layer):
        own = place.rank()
        pltpu.make_async_copy(
            cut.at[layer, own], pasted.at[layer, own], trade_sems.at[0, layer, 0]
        ).wait()
        for e in range(1, PLANE):
            traded(layer, e).wait_recv()
        for e in range(1, PLANE):
            trade(layer, e).wait_send()
        for m, low in ((0, 0), (2, q_cols)):
            width = slabs[m].shape[2]
            whole = [pasted[layer, t, :rows, low : low + width].astype(F32) for t in range(PLANE)]
            slabs[m][layer, rows_of(m, z), :] = jnp.concatenate(whole, axis=0).astype(BF)

    trades = place.trades(levels)
    o_trade = remote(
        o_cut, o_piece, o_sems.at[0], o_sems.at[1], place.indexed(place.holder(levels))
    )
    o_local = pltpu.make_async_copy(o_cut, o_piece, o_sems.at[0])

    def mask_to(e):
        there = mask.at[place.y, place.x, :, place.core]
        return remote(own_mask, there, mask_sems.at[0, e], mask_sems.at[1, e], place.other(e))

    def mask_from(e):
        y, core, x = place.turned(e)
        there = mask.at[y, x, :, core]
        return remote(there, there, mask_sems.at[0, e], mask_sems.at[1, e], place.other(e))

    mask_local = pltpu.make_async_copy(
        own_mask, mask.at[place.y, place.x, :, place.core], mask_sems.at[0, 0]
    )

    middle = (z == 1) | (z == 2)

    def relay_on(layer, m):
        if relayed:
            @pl.when(middle)
            def _():
                arriving(layer, m, 2).wait_recv()
                relay(layer, m).start()

    def weights_here(layer, m):
        for delta in range(1, levels):
            if relayed and delta == 2:
                pl.when(jnp.logical_not(middle))(arriving(layer, m, delta).wait_recv)
            else:
                arriving(layer, m, delta).wait_recv()
        for_spread(layer, m, lambda copy: copy.wait_send())
        if m % 2:
            own_piece(layer, m).wait()
        if relayed:
            pl.when(middle)(relay(layer, m).wait_send)

        return keep(slabs[m].at[layer], slab_outs[m].at[layer])

    skip = slabs[2].at[0, :, : adjoint.shape[3]]
    loads = [
        pltpu.make_async_copy(src, dst, load_sems.at[i])
        for i, (src, dst) in enumerate(zip(head_weights, (first, final, skip)))
    ]
    loads[0].start()
    loads[1].start()
    greet(place, levels)

    g_own = g.at[place.y, :, :, place.core]
    g_far = g.at[1 - place.y, :, :, place.core]
    g_local = pltpu.make_async_copy(adjoint, g_own, g_sems.at[0, 0])
    g_peer = remote(adjoint, g_own, g_sems.at[0, 1], g_sems.at[1, 1], place.far(0))
    g_sibling = remote(adjoint, g_own, g_sems.at[0, 2], g_sems.at[1, 2], place.sibling())
    g_pass = remote(g_far, g_far, g_sems.at[0, 3], g_sems.at[1, 3], place.sibling())
    part = exchange[0]
    lines = nrm.at[0]
    bufs = [nrm.at[0], nml.at[0], nrm.at[1], nml.at[1], lines]
    phases = [Exchange(place, p, buf, exchange) for p, buf in enumerate(bufs)]

    def own_half(s):
        return slice(s * HALF_BLOCK, (s + 1) * HALF_BLOCK)

    def chip_of(s, major, minor):
        return (major + s * (minor - major), minor + s * (major - minor))

    def enter(p, s, values):
        if p < 2 * LAYERS:
            values = values * root(values)
        bufs[p][phases[p].own(s)] = values.astype(BF)
        phases[p].start(s)

    def leave(p, s):
        rows = own_half(s)
        total = phases[p].total(s)
        if p == 2 * LAYERS:
            grad_out[rows, :] = total
            return
        layer = p // 2
        if p % 2 == 0:
            values = xs[layer, rows, :] + total
            mid[layer, rows, :] = values
        else:
            values = mid[layer, rows, :] + total
            if layer + 1 < LAYERS:
                xs[layer + 1, rows, :] = values
        enter(p + 1, s, values)

    def run(p, compute, next_weights, more=()):
        more = list(more)
        hooks = [(1, lambda: leave(p - 1, 1))] if p else []
        hooks += [(2, lambda key=key: relay_on(*key)) for key in next_weights]
        phases[p].run(compute, hooks + more)
        leave(p, 0)
        phases[p].near_stage(1)

    o_cut[...] = jnp.zeros(o_cut.shape, BF)
    for layer in range(LAYERS):
        o_cut[layer, :rows, :] = w_out[layer]
    pl.when(trades)(o_trade.start)
    pl.when(jnp.logical_not(trades))(o_local.start)
    cut_weights(0)
    start_trade(0)
    cut_weights(1)
    end_trade(0)
    send_weights(0, 0)
    xs[0] = x_in[...].astype(F32)
    for s in range(2):
        enter(0, s, xs[0, own_half(s), :])
    mask_local.start()
    for e in range(1, PLANE):
        mask_to(e).start()

    @pl.when(trades)
    def _():
        o_trade.wait_recv()
        o_trade.wait_send()

    pl.when(jnp.logical_not(trades))(o_local.wait)
    send_weights(0, 1)
    start_trade(1)
    for copy in (g_local, g_peer, g_sibling):
        copy.start()
    mask_local.wait()
    for e in range(1, PLANE):
        mask_from(e).wait_recv()
        mask_to(e).wait_send()
    relay_on(0, 0)
    relay_on(0, 1)

    def second_layer():
        end_trade(1)
        send_weights(1, 0)
        send_weights(1, 1)

    slab_keeps = []
    for layer in range(LAYERS):
        wq, wo, wi, wd = [slab.at[layer] for slab in slabs]
        slab_keeps.append(weights_here(layer, 0))
        if layer == 0:
            send_weights(0, 2)
            send_weights(0, 3)
        for n in range(0, wide_q.shape[0], 256):
            wide_q[n : n + 256, :] = dot(wq[n : n + 256, :], sel_q[...]).astype(BF)
        slab_keeps.append(weights_here(layer, 1))
        if layer:
            for copy in attn_saved:
                forget(copy)

        def attend(start, s, half, major, layer=layer, wo=wo):
            both = rows_at(start, 2 * BLOCK, 2 * BLOCK)
            projected = dot(nrm[layer, s, major].reshape(2 * BLOCK, nrm.shape[-1]), wide_q[...])
            cosine, sine = rope[:, :BLOCK], rope[:, BLOCK:]
            allowed = [
                mask[chip_of(s, major, block) + (s,)].reshape(BLOCK, BLOCK) > 0 for block in range(2)
            ]
            units = [(block, h) for block in range(2) for h in range(heads)]
            turned = []
            for low in range(0, 2 * lanes, BLOCK):
                value = projected[:, low : low + BLOCK]
                value = value * cosine + pltpu.roll(value, BLOCK // 2, 1) * sine
                turned.append(value.astype(BF))
            values = projected[:, 2 * lanes :].astype(BF)

            def rows_in(array, block):
                return array[block * BLOCK : (block + 1) * BLOCK]

            scores = [
                dot(rows_in(turned[h], block), rows_in(turned[heads + h], block), 1, 1)
                for block, h in units
            ]
            scores = [
                jnp.where(allowed[block], score * (1.0 / math.sqrt(HDIM)), -1e30)
                for (block, h), score in zip(units, scores)
            ]
            tops = [jnp.max(score, axis=-1, keepdims=True) for score in scores]
            scores = [jnp.exp(score - top) for score, top in zip(scores, tops)]
            sums = [jnp.sum(score, axis=-1, keepdims=True) for score in scores]
            probs = [(score / total).astype(BF) for score, total in zip(scores, sums)]
            outs = [
                dot(prob, rows_in(values, block)[:, h * BLOCK : (h + 1) * BLOCK]).astype(BF)
                for (block, h), prob in zip(units, probs)
            ]

            def joined(parts):
                side = [
                    jnp.concatenate(parts[block * heads : (block + 1) * heads], axis=1)
                    for block in range(2)
                ]
                return jnp.concatenate(side, axis=0)

            attended = dot(joined(outs), sel_o[...], 1, 1).astype(BF)
            write_part(part, s, half, attended, wo, 0)
            att[both, :] = attended
            prb[both, :] = joined(probs)
            qkv[both, :] = jnp.concatenate(turned + [values], axis=1)

        more = [(1, second_layer)] if layer == 0 else []
        run(2 * layer, attend, ((layer, 2), (layer, 3)), more)
        attn_saved = [keep(src, dst.at[layer]) for src, dst in zip((qkv, prb, att), kept[2:5])]
        nrm_saved = keep(nrm.at[layer], kept[0].at[layer])
        if layer == 0:
            g_peer.wait_recv()
            g_pass.start()
        ending = layer + 1 == LAYERS
        slab_keeps.append(weights_here(layer, 2))
        if layer:
            for copy in mlp_saved:
                forget(copy)
        slab_keeps.append(weights_here(layer, 3))
        if not ending:
            for m in (2, 3):
                send_weights(layer + 1, m)

        def lift(start, s, major, layer=layer, wi=wi):
            rows = rows_at(start, 2 * BLOCK, 2 * BLOCK)
            lifted = dot(nml[layer, s, major].reshape(2 * BLOCK, nml.shape[-1]), wi[...])
            root_two = math.sqrt(2.0 / math.pi)
            square = lifted * lifted
            tanh = jnp.tanh(root_two * lifted * (1.0 + 0.044715 * square))
            activated = (0.5 * lifted * (1.0 + tanh)).astype(BF)
            act[rows, :] = activated
            slope = 0.5 * (1.0 + tanh) + 0.5 * lifted * (1.0 - tanh * tanh) * root_two * (
                1.0 + 3.0 * 0.044715 * square
            )
            gl[rows, :] = slope.astype(BF)
            return activated

        def perceptron(start, s, half, major, lift=lift, wd=wd):
            write_part(part, s, half, lift(start, s, major), wd, 0)

        following = () if ending else ((layer + 1, 0), (layer + 1, 1))
        run(2 * layer + 1, perceptron, following)
        mlp_saved = [keep(src, dst.at[layer]) for src, dst in zip((gl, act), kept[5:7])]
        keep(nml.at[layer], kept[1].at[layer])
        if layer == 0:
            forget(nrm_saved)
            forget(slab_keeps[2])
            loads[2].start()
            loads[0].wait()
            loads[1].wait()
            index = lax.broadcasted_iota(jnp.int32, pick.shape, 0)
            offset = (2 * place.y + place.core) * (pick.shape[0] // (4 * levels))
            pick[...] = jnp.where(index - offset == head_lanes[...], 1.0, 0.0).astype(BF)
            for n in range(0, first.shape[0], 256):
                first_q[n : n + 256, :] = dot(first[n : n + 256, :], pick[...]).astype(BF)
            final_q[...] = dot(pick[...], final[...], 0, 0).astype(BF)

    g_local.wait()
    for copy in (g_sibling, g_pass):
        copy.wait_recv()
    loads[2].wait()
    bias_q = dot(jnp.broadcast_to(bias_first[...], (16, bias_first.shape[1])), pick[...])[:1]
    columns = g.shape[-1]

    def head(start, s, half, major):
        rows = rows_at(start, 2 * BLOCK, 2 * BLOCK)
        pre = dot(lines[s, major].reshape(2 * BLOCK, lines.shape[-1]), first_q[...]) + bias_q
        gate = 1.0 / (1.0 + jnp.exp(-pre))
        hidden[rows, :] = (pre * gate).astype(BF)
        for block in range(2):
            here = rows_at(start + block * BLOCK, BLOCK, BLOCK)
            g_rows[here, :] = g[chip_of(s, major, block) + (s,)].reshape(BLOCK, columns)
        there = g_rows[rows, :]
        grad_hidden = dot(there, final_q[...], 1, 1)
        gpre[rows, :] = (grad_hidden * (gate * (1.0 + pre * (1.0 - gate)))).astype(BF)
        row = lax.broadcasted_iota(jnp.int32, (2 * BLOCK, 1), 0)
        y = major + s * (row // BLOCK - major)
        mine = (row // HALF_BLOCK % 2 == place.core) & (y == place.y)
        mine = jnp.where(mine, there.astype(F32), 0.0).astype(BF)
        whole = dot(gpre[rows, :], first_q[...], 1, 1) + dot(mine, skip[...], 1, 1)
        part[s, half] = blocked(whole.astype(BF))

    p = 2 * LAYERS
    phases[p].run(head, [(1, lambda: leave(p - 1, 1))])

    keep(lines, kept[7])
    keep(hidden, kept[8])
    keep(gpre, kept[9])
    keep(g_rows, kept[11])
    for s in range(2):
        for major in range(2):
            n = (2 * s + major) * 2 * BLOCK
            rows = lines[s, major].reshape(2 * BLOCK, lines.shape[-1])
            picked[n : n + 2 * BLOCK, :] = dot(rows, pick[...]).astype(BF)
    keep(picked, kept[10])
    phases[p].near_stage(1)
    mine = []
    for x in range(2):
        mine += [lines[0, place.y, x, place.core], lines[1, x, place.y, place.core]]
    mine = jnp.concatenate(mine, axis=0)
    pre = dot(mine, first[...]) + bias_first[...].astype(F32)
    hidden_all[...] = (pre / (1.0 + jnp.exp(-pre))).astype(BF)
    out = dot(hidden_all[...], final[...]) + bias_last[...].astype(F32)
    predictions[...] = (out + dot(mine, skip[...])).astype(BF)
    leave(p, 0)
    leave(p, 1)
    for copy in (g_peer, g_sibling, g_pass):
        copy.wait_send()
    for copy in kept_here:
        if not any(copy is other for other in waited):
            copy.wait()


def norm_back(values, q):
    scale = root(values)
    n = values * scale
    return scale * (q - n * jnp.mean(q * n, axis=-1, keepdims=True))


def backward_kernel(levels, *refs):
    (rope, sel_q, sel_o, gains, w_q, w_in) = refs[:6]
    dy_in, stored, head_stored = refs[6], refs[7:20], refs[20:25]
    (dx_out, small_out, q_out, o_out, i_out, d_out, q_gain, i_gain) = refs[25:33]
    (first_out, out_out, skip_out) = refs[33:36]
    exchange, ag = refs[36:43], refs[43]
    loaded, gp = refs[44:57], refs[57]
    stages, arrivals = refs[58:65], refs[65:72]
    own_sums, acc, o_acc = refs[72:76], refs[76], refs[77]
    o_cut, o_pasted = refs[78], refs[79]
    (small_own, small_x, small_z) = refs[80:83]
    row_buf = refs[83]
    z_sems, load_sems, small_sems, trade_sems, o_sems, row_sem = refs[84:]
    (nml, act, gl, wi, wd, mid, nrm, qkv, prb, att, wq, wo, xs) = loaded
    part = exchange[0]
    place = Place()
    z = place.z
    heads = sel_o.shape[1] // BLOCK
    lanes = heads * BLOCK

    def load(layer, i):
        return pltpu.make_async_copy(stored[i].at[layer], loaded[i], load_sems.at[i])

    lines = ag.at[1]
    h_cols, half_width = small_own.shape[2], nrm.shape[-1] // 2
    gpre, hidden = gp.at[:, :h_cols], nrm.at[:, :, :, :, :, :h_cols]
    picked = nrm.at[:, :, :, :, :, half_width : half_width + h_cols]
    g = qkv.at[:, : stages[5].shape[1]]
    head_loads = [
        pltpu.make_async_copy(src, dst, load_sems.at[len(loaded) + i])
        for i, (src, dst) in enumerate(zip(head_stored, (lines, gpre, hidden, picked, g)))
    ]
    mlp_part, attn_part = range(5), range(6, 12)
    norm_loads = [pltpu.make_async_copy(stored[i], loaded[i], load_sems.at[i]) for i in (5, 12)]
    for copy in norm_loads:
        copy.start()
    dy_load = pltpu.make_async_copy(dy_in, dx_out, load_sems.at[len(loaded) + 5])
    dy_load.start()
    for copy in head_loads:
        copy.start()
    for i in mlp_part:
        load(LAYERS - 1, i).start()
    greet(place, levels)

    def count_of(m):
        return arrivals[m].shape[2]

    def slot(m, layer):
        return layer if m < 4 else 0

    relayed = levels == 4
    middle = (z == 1) | (z == 2)

    def send(layer, m, delta):
        there = (z + delta) % levels
        return remote(
            stages[m].at[rows_at(there * count_of(m), count_of(m))],
            arrivals[m].at[slot(m, layer), delta - 1],
            z_sems.at[0, layer, m, delta - 1],
            z_sems.at[1, layer, m, delta - 1],
            place.level(there),
        )

    def far(delta):
        there = (z + delta) % levels
        return (z + there == 3) & (z * there == 0)

    def hand(layer, m, delta):
        there = (z + delta) % levels
        return remote(
            stages[m].at[rows_at(there * count_of(m), count_of(m))],
            arrivals[m].at[slot(m, layer), levels - 1],
            z_sems.at[0, layer, m, delta - 1],
            z_sems.at[1, layer, m, levels - 1],
            place.level(1 + z // 3),
        )

    def send_first(layer, m):
        for delta in range(1, levels):
            if not relayed:
                send(layer, m, delta).start()
            elif delta == 2:
                pl.when(jnp.logical_not(middle))(send(layer, m, delta).start)
            else:
                pl.when(far(delta))(hand(layer, m, delta).start)
                pl.when(jnp.logical_not(far(delta)))(send(layer, m, delta).start)

    def send_rest(layer, m):
        if relayed:
            @pl.when(middle)
            def _():
                hand(layer, m, 1).wait_recv()
                rows = rows_at((z + 2) % levels * count_of(m), count_of(m))
                total = stages[m][rows, :].astype(F32)
                total = total + arrivals[m][slot(m, layer), levels - 1].astype(F32)
                stages[m][rows, :] = total.astype(BF)
                send(layer, m, 2).start()

    def sent(layer, m):
        for delta in range(1, levels):
            send(layer, m, delta).wait_send()

    def result(layer, m):
        if m > 4:
            return (out_out, skip_out)[m - 5]
        if m == 3:
            return d_out.at[layer]
        return own_sums[min(m, 3)].at[slot(m, layer)]

    def weight_grad(layer, m, left, right, tile):
        width = left.shape[-1]
        if m < 4 and layer + 1 < LAYERS:
            sent(layer + 1, m)
        for low in range(0, width, tile):
            here = slice(low, min(low + tile, width))
            stages[m][here, :] = dot(flat(left, here), flat(right), 0, 0).astype(BF)
        send_first(layer, m)
        out = result(layer, m)
        out[...] = stages[m][rows_at(z * count_of(m), count_of(m)), :].astype(out.dtype)

    bufs = [ag.at[p % 2] for p in range(PHASES)]
    phases = [Exchange(place, p, buf, exchange) for p, buf in enumerate(bufs)]

    def own_half(s):
        return slice(s * HALF_BLOCK, (s + 1) * HALF_BLOCK)

    def enter(p, s):
        bufs[p][phases[p].own(s)] = dx_out[own_half(s), :].astype(BF)
        phases[p].start(s)

    def leave(p, s):
        rows = own_half(s)
        values = (mid if p % 2 == 0 else xs)[LAYERS - 1 - p // 2, rows, :]
        dx_out[rows, :] += norm_back(values, phases[p].total(s))
        if p + 1 < PHASES:
            enter(p + 1, s)

    def run(p, compute, relays):
        hooks = [(1, lambda: leave(p - 1, 1))] if p else []
        hooks += [(2, lambda key=key: send_rest(*key)) for key in relays]
        phases[p].run(compute, hooks)

    dy_load.wait()
    for copy in norm_loads:
        copy.wait()
    for s in range(2):
        enter(0, s)

    for copy in head_loads:
        copy.wait()
    last = LAYERS - 1
    bias_sum = jnp.sum(gpre[...].astype(F32), axis=0, keepdims=True)
    small_own[1] = jnp.broadcast_to(bias_sum, small_own.shape[1:])
    to_x = remote(
        small_own.at[1], small_x, small_sems.at[0, 0], small_sems.at[1, 0], place.near(0)
    )
    to_x.start()
    weight_grad(last, 5, hidden, g, 4 * BLOCK)
    weight_grad(last, 6, picked, g, 4 * BLOCK)
    weight_grad(last, 4, lines, gpre, 5 * BLOCK)
    g_sum = jnp.sum(g[...].astype(F32), axis=0, keepdims=True)
    to_x.wait()
    small_z[0, :, : g_sum.shape[1]] = jnp.broadcast_to(g_sum, (8, g_sum.shape[1]))
    small_z[0, :, g_sum.shape[1] :] = small_own[1] + small_x[...]
    to_z = [
        remote(
            small_z.at[0], small_z.at[d], small_sems.at[0, d], small_sems.at[1, d],
            place.level((z + d) % levels),
        )
        for d in range(1, levels)
    ]
    for copy in to_z:
        copy.start()
    for i in attn_part:
        load(last, i).start()

    relays = [(last, 5), (last, 6), (last, 4)]
    for layer in reversed(range(LAYERS)):
        p = 2 * (LAYERS - 1 - layer)
        buf = bufs[p]
        for i in mlp_part:
            load(layer, i).wait()

        def perceptron(start, s, half, major, buf=buf):
            rows = rows_at(start, 2 * BLOCK, 2 * BLOCK)
            grad_act = dot(buf[s, major].reshape(2 * BLOCK, buf.shape[-1]), wd[...], 1, 1)
            grad_lift = (grad_act * gl[rows, :].astype(F32)).astype(BF)
            write_part(part, s, half, grad_lift, wi, 1)
            gl[rows, :] = grad_lift

        run(p, perceptron, relays)
        weight_grad(layer, 3, act, buf, 2 * BLOCK)
        leave(p, 0)
        weight_grad(layer, 2, nml, gl, 5 * BLOCK)
        phases[p].near_stage(1)
        if layer > 0:
            for i in mlp_part:
                load(layer - 1, i).start()
        for i in attn_part:
            load(layer, i).wait()
        buf = bufs[p + 1]

        def attend(start, s, half, major, buf=buf):
            cosine, sine = rope[:, :BLOCK], rope[:, BLOCK:]
            both = rows_at(start, 2 * BLOCK, 2 * BLOCK)
            there = buf[s, major].reshape(2 * BLOCK, buf.shape[-1])
            grad_heads = dot(there, wo[...], 1, 1).astype(BF)
            grad_heads = dot(grad_heads, sel_o[...]).astype(BF)
            kept, probs = qkv[both, :], prb[both, :]
            units = [(block, h) for block in range(2) for h in range(heads)]

            def unit(array, block, h, kind=0):
                low = kind * lanes + h * BLOCK
                return array[block * BLOCK : (block + 1) * BLOCK, low : low + BLOCK]

            queries, keys, values = [[unit(kept, *u, kind) for u in units] for kind in range(3)]
            probs = [unit(probs, *u) for u in units]
            grads = [unit(grad_heads, *u) for u in units]
            grad_probs = [dot(grad, value, 1, 1) for grad, value in zip(grads, values)]
            grad_values = [dot(prob, grad, 0, 0).astype(BF) for prob, grad in zip(probs, grads)]
            wide = [prob.astype(F32) for prob in probs]
            inner = [
                jnp.sum(prob * grad, axis=-1, keepdims=True) for prob, grad in zip(wide, grad_probs)
            ]
            grad_scores = [
                (prob * (grad - total)).astype(BF)
                for prob, grad, total in zip(wide, grad_probs, inner)
            ]
            grad_queries = [dot(grad, key) for grad, key in zip(grad_scores, keys)]
            grad_keys = [dot(grad, query, 0, 0) for grad, query in zip(grad_scores, queries)]
            packed = []
            for parts in (grad_queries, grad_keys):
                for h in range(heads):
                    turned = jnp.concatenate([parts[h], parts[heads + h]], axis=0)
                    turned = turned * (1.0 / math.sqrt(HDIM))
                    turned = turned * cosine - pltpu.roll(turned, BLOCK // 2, 1) * sine
                    packed.append(turned.astype(BF))
            for h in range(heads):
                packed.append(jnp.concatenate([grad_values[h], grad_values[heads + h]], axis=0))
            packed = dot(jnp.concatenate(packed, axis=1), sel_q[...], 1, 1).astype(BF)
            write_part(part, s, half, packed, wq, 1)
            gp[both, :] = packed

        run(p + 1, attend, [(layer, 3), (layer, 2)])
        weight_grad(layer, 0, nrm, gp, 5 * BLOCK)
        leave(p + 1, 0)
        weight_grad(layer, 1, att, buf, 2 * BLOCK)
        phases[p + 1].near_stage(1)
        if layer > 0:
            for i in attn_part:
                load(layer - 1, i).start()
        relays = [(layer, 0), (layer, 1)]
    leave(PHASES - 1, 1)
    for key in relays:
        send_rest(*key)

    total = small_z[0]
    for copy, d in zip(to_z, range(1, levels)):
        copy.wait_recv()
        total = total + small_z[d]
    small_out[...] = total
    for copy in to_z:
        copy.wait_send()
    rows = w_q.shape[1]
    pad_rows = up16(rows)
    kinds = {0: 0, 2: 1, 4: 2}

    def cut_at(m, t):
        start = rows_at((t + PLANE * kinds[m]) * pad_rows, pad_rows)
        return wi.at[start, : stages[m].shape[1]]

    def pasted_at(layer, m, t):
        start = rows_at((slot(m, layer) * PLANE + t) * pad_rows, pad_rows)
        return {0: gl, 2: act, 4: wd}[m].at[start, : stages[m].shape[1]]

    def trade(layer, m, e):
        kind = kinds[m]
        return remote(
            cut_at(m, place.rank(e)), pasted_at(layer, m, place.rank()),
            trade_sems.at[0, layer, kind, e], trade_sems.at[1, layer, kind, e], place.other(e),
        )

    def traded(layer, m, e):
        there = pasted_at(layer, m, place.rank(e))
        return remote(
            there, there, trade_sems.at[0, layer, kinds[m], e],
            trade_sems.at[1, layer, kinds[m], e], place.other(e),
        )

    def own_trade(layer, m):
        own = place.rank()
        return pltpu.make_async_copy(
            cut_at(m, own), pasted_at(layer, m, own), trade_sems.at[0, layer, kinds[m], 0]
        )

    stayed = set()

    def wait_own_trade(layer, m):
        if (layer, m) not in stayed:
            own_trade(layer, m).wait()
            stayed.add((layer, m))

    def pasted(layer, m, t):
        return pasted_at(layer, m, t)[:rows, :].astype(F32)

    trades = place.trades(levels)

    def o_trade(layer):
        return remote(
            o_cut.at[layer], o_pasted.at[layer], o_sems.at[0, layer], o_sems.at[1, layer],
            place.indexed(place.held(levels)),
        )

    def o_local(layer):
        return pltpu.make_async_copy(o_cut.at[layer], o_pasted.at[layer], o_sems.at[0, layer])

    def finalize(layer, m):
        own = result(layer, m)
        if m == 3 or m > 4:
            total = own
        else:
            total = o_acc if m == 1 else acc.at[:, : own.shape[1]]
            total[...] = own[...].astype(F32)
        for delta in range(1, levels):
            def add(delta=delta):
                send(layer, m, delta).wait_recv()
                total[...] += arrivals[m][slot(m, layer), delta - 1].astype(F32)

            if relayed and delta != 2:
                source = (z + levels - delta) % levels
                pl.when(jnp.logical_not((z + source == 3) & (z * source == 0)))(add)
            else:
                add()
        if m > 3 or layer == 0:
            sent(layer, m)
        if m == 1:
            o_cut[layer] = total[...].astype(BF)
            pl.when(trades)(o_trade(layer).start)
            pl.when(jnp.logical_not(trades))(o_local(layer).start)
        elif m in kinds:
            if m < 4 and layer + 1 < LAYERS:
                wait_own_trade(layer + 1, m)
                for e in range(1, PLANE):
                    trade(layer + 1, m, e).wait_send()
            values = total[...].astype(BF).astype(F32)
            for t in range(PLANE):
                cut_at(m, t)[:rows, :] = values[t * rows : (t + 1) * rows].astype(BF)
            own_trade(layer, m).start()
            for e in range(1, PLANE):
                trade(layer, m, e).start()

    def wait_trade(layer, m):
        wait_own_trade(layer, m)
        for e in range(1, PLANE):
            traded(layer, m, e).wait_recv()
        if m > 3 or layer == 0:
            for e in range(1, PLANE):
                trade(layer, m, e).wait_send()

    span = w_q.shape[2] // 3 // PLANE
    ff_rows = w_in.shape[2] // PLANE // levels
    padded_rows = stages[2].shape[1] // levels

    def rows_out(layer, out):
        here = row_buf.at[:, : out.shape[2]]
        return pltpu.make_async_copy(here, out.at[layer], row_sem.at[0])

    on_the_way = []

    def write_rows(layer, parts, out, kind, w, gain_out):
        whole = jnp.concatenate(parts, axis=1)
        gain_out[layer] = jnp.sum(whole * w[layer].astype(F32), axis=1, keepdims=True)
        if on_the_way:
            on_the_way.pop().wait()
        row_buf[:, : out.shape[2]] = whole * gains[kind, layer]
        copy = rows_out(layer, out)
        copy.start()
        on_the_way.append(copy)

    def assemble(layer):
        wait_trade(layer, 0)
        ranks = [pasted(layer, 0, t) for t in range(PLANE)]
        parts = [rank[:, kind * span : (kind + 1) * span] for kind in range(3) for rank in ranks]
        write_rows(layer, parts, q_out, 0, w_q, q_gain)

    def assemble_mlp(layer):
        wait_trade(layer, 2)
        ranks = [pasted(layer, 2, t) for t in range(PLANE)]
        parts = [
            rank[:, zz * padded_rows : zz * padded_rows + ff_rows]
            for zz in range(levels) for rank in ranks
        ]
        write_rows(layer, parts, i_out, 1, w_in, i_gain)

    def assemble_out(layer):
        @pl.when(trades)
        def _():
            o_trade(layer).wait_recv()
            o_trade(layer).wait_send()

        pl.when(jnp.logical_not(trades))(o_local(layer).wait)
        o_out[layer] = o_pasted[layer, :rows, :].astype(F32)

    head_rows, head_share = out_out.shape[0], first_out.shape[1] // 4 // levels

    def assemble_head():
        wait_trade(last, 4)
        sums = []
        for q in range(4):
            sums.append(pasted(last, 4, 2 * q) + pasted(last, 4, 2 * q + 1))
        parts = []
        for zz in range(levels):
            for q in range(4):
                parts.append(sums[q][:, zz * head_rows : zz * head_rows + head_share])
        first_out[...] = jnp.concatenate(parts, axis=1)

    for key in [(last, 5), (last, 6), (last, 4)] + [(last, m) for m in (3, 2, 0, 1)]:
        finalize(*key)
    for layer in reversed(range(LAYERS - 1)):
        finalize(layer, 3)
        finalize(layer, 2)
    assemble_head()
    for layer in reversed(range(LAYERS - 1)):
        finalize(layer, 0)
        finalize(layer, 1)
    for layer in reversed(range(LAYERS)):
        assemble_mlp(layer)
        assemble(layer)
        assemble_out(layer)
    on_the_way.pop().wait()


def shape(*dims, dtype=BF):
    return jax.ShapeDtypeStruct(dims, dtype)


def rope_table():
    position = np.arange(2 * BLOCK) % ROW_LEN
    inverse = ROTARY_BASE ** (-np.arange(HALF) / HALF)
    angles = (position[:, None] * inverse[None, :]).astype(np.float32)
    table = np.zeros((2 * BLOCK, 2, 2, BLOCK // 2), np.float32)
    table[:, 0, :, :HALF] = np.cos(angles)[:, None]
    table[:, 1, 0, :HALF] = -np.sin(angles)
    table[:, 1, 1, :HALF] = np.sin(angles)
    return table.reshape(2 * BLOCK, 2 * BLOCK)


def lane_of(index):
    head, inside = divmod(index, HDIM)
    half, place = divmod(inside, HALF)
    return head * BLOCK + half * (BLOCK // 2) + place


def per_device(devices, x, segments, padded, w_qkv, w_out, w_in, w_down, gain_attn, gain_mlp,
               head_first, head_first_bias, head_final, head_bias, head_skip, adjoint):
    levels = devices // PLANE
    width = x.shape[1]
    ff = w_in.shape[2]
    columns = head_final.shape[1]
    tokens = PLANE * BLOCK
    heads = width // HDIM // PLANE
    span = heads * HDIM
    rows = width // devices
    out_rows = up16(rows)
    ff_rows = ff // devices
    down_rows = up16(ff_rows)
    head_share = 2 * width // devices
    head_rows = up16(head_share)
    used_cols, o_rows, f_cols = 3 * span, levels * out_rows, levels * down_rows
    h_cols = -(-levels * head_rows // 128) * 128
    q_cols = -(-used_cols // 128) * 128
    lanes = heads * BLOCK

    sel_q = np.zeros((q_cols, 3 * lanes), np.float32)
    sel_o = np.zeros((o_rows, lanes), np.float32)
    for e in range(span):
        for kind in range(3):
            sel_q[kind * span + e, kind * lanes + lane_of(e)] = 1
        sel_o[e // rows * out_rows + e % rows, lane_of(e)] = 1
    sel_q, sel_o = jnp.asarray(sel_q, BF), jnp.asarray(sel_o, BF)
    rope = jnp.asarray(rope_table())
    head_lanes = np.full((1, h_cols), -width, np.int32)
    for zz in range(levels):
        here = slice(zz * head_rows, zz * head_rows + head_share)
        head_lanes[0, here] = 4 * head_share * zz + np.arange(head_share)
    head_lanes = jnp.asarray(head_lanes)

    seg = segments.reshape(2, HALF_BLOCK)
    open_key = padded.reshape(2, HALF_BLOCK) == 0
    within = jnp.arange(HALF_BLOCK)
    static = within[:, None] // ROW_LEN == within[None, :] // ROW_LEN
    static = static & (within[None, :] <= within[:, None])
    allowed = static[None] & (seg[:, :, None] == seg[:, None, :])
    allowed = allowed & (open_key[:, None, :] | (within[:, None] == within[None, :])[None])
    core = lax.axis_index("wide") % 2
    side = jnp.arange(BLOCK)[None, None, :] // HALF_BLOCK == core
    own_mask = (jnp.concatenate([allowed, allowed], axis=-1) & side).astype(BF)

    gains = jnp.stack([gain_attn, gain_mlp]).astype(F32)[..., None]
    d_piece = w_down
    if down_rows != ff_rows:
        d_piece = jnp.pad(w_down, [(0, 0), (0, down_rows - ff_rows), (0, 0)])
    pad_rows = up16(rows)

    in_blocks = (2, 2, 2, 2, HALF_BLOCK)
    layer_shapes = [
        in_blocks + (width,), in_blocks + (width,), (tokens, 3 * lanes), (tokens, lanes), (tokens, o_rows),
        (tokens, f_cols), (tokens, f_cols),
    ]
    slab_shapes = [(width, q_cols), (o_rows, width), (width, f_cols), (f_cols, width)]
    outs = [
        shape(2 * BLOCK, columns), shape(BLOCK, width, dtype=F32),
        shape(LAYERS, BLOCK, width, dtype=F32), shape(LAYERS, BLOCK, width, dtype=F32),
    ]
    vmem_outs = len(outs)
    outs += [shape(LAYERS, *dims) for dims in layer_shapes]
    outs += [shape(*in_blocks, width)] + [shape(tokens, h_cols)] * 3 + [shape(tokens, columns)]
    outs += [shape(LAYERS, *dims) for dims in slab_shapes]
    (predictions, grad_final, xs, mid, nrm, nml, qkv, prb, att, gl, act, lines, hidden, gpre,
     picked, g, wq, wo, wi, wd) = pl.pallas_call(
        lambda *refs: forward_kernel(levels, *refs),
        out_shape=outs,
        in_specs=[VMEM] * 13 + [ANY] * 4,
        out_specs=[VMEM] * vmem_outs + [ANY] * (len(outs) - vmem_outs),
        scratch_shapes=exchange_scratch(width, PHASES + 1)
        + [pltpu.VMEM((LAYERS,) + dims, BF) for dims in layer_shapes[:2]]
        + [pltpu.VMEM(dims, BF) for dims in layer_shapes[2:]]
        + [pltpu.VMEM((LAYERS,) + dims, BF) for dims in slab_shapes]
        + [
            pltpu.VMEM((width, 3 * lanes), BF), pltpu.VMEM((width, width), BF),
            pltpu.VMEM((width, columns), BF), pltpu.VMEM((width, h_cols), BF),
            pltpu.VMEM((width, h_cols), BF), pltpu.VMEM((h_cols, columns), BF),
            pltpu.VMEM(in_blocks + (columns,), BF), pltpu.VMEM((tokens, columns), BF),
            pltpu.VMEM((tokens, h_cols), BF),
            pltpu.VMEM((tokens, h_cols), BF), pltpu.VMEM((tokens, h_cols), BF),
            pltpu.VMEM((2 * BLOCK, width), BF),
            pltpu.VMEM(in_blocks + (BLOCK,), BF),
            pltpu.VMEM((LAYERS, PLANE, pad_rows, q_cols + f_cols), BF),
            pltpu.VMEM((LAYERS, PLANE, pad_rows, q_cols + f_cols), BF),
            pltpu.VMEM((LAYERS, out_rows, width), BF),
            pltpu.VMEM((LAYERS, out_rows, width), BF),
            pltpu.SemaphoreType.DMA((3, LAYERS, 4, levels - 1)),
            pltpu.SemaphoreType.DMA((LAYERS, 4)),
            pltpu.SemaphoreType.DMA((32,)),
            pltpu.SemaphoreType.DMA((3,)),
            pltpu.SemaphoreType.DMA((2, 4)),
            pltpu.SemaphoreType.DMA((2, LAYERS, PLANE)),
            pltpu.SemaphoreType.DMA((2, PLANE)),
            pltpu.SemaphoreType.DMA((2,)),
        ],
        compiler_params=pltpu.CompilerParams(
            collective_id=1, has_side_effects=True, vmem_limit_bytes=62 * MIB
        ),
        name="decoder_forward",
    )(x, own_mask, rope, sel_q, sel_o, head_lanes,
      adjoint.reshape(2, 2, HALF_BLOCK, columns), head_first_bias[None], head_bias[None], gains,
      w_qkv, w_in, w_out, d_piece, head_first, head_final, head_skip)

    chunk = [PLANE * rows, out_rows, PLANE * rows, down_rows, PLANE * rows, head_rows, head_rows]
    cols = [q_cols, width, f_cols, width, h_cols, columns, columns]
    stage_rows = [levels * n for n in chunk[:5]] + [h_cols] * 2
    kept_shapes = [
        in_blocks + (width,), (tokens, f_cols), (tokens, f_cols), (width, f_cols), (f_cols, width),
        (LAYERS, BLOCK, width), in_blocks + (width,), (tokens, 3 * lanes), (tokens, lanes),
        (tokens, o_rows), (width, q_cols), (o_rows, width), (LAYERS, BLOCK, width),
    ]
    small_cols = columns + h_cols
    outs = [
        shape(BLOCK, width, dtype=F32), shape(8, small_cols, dtype=F32),
        shape(LAYERS, rows, 3 * width, dtype=F32), shape(LAYERS, rows, width, dtype=F32),
        shape(LAYERS, rows, ff, dtype=F32), shape(LAYERS, down_rows, width, dtype=F32),
        shape(LAYERS, rows, 1, dtype=F32), shape(LAYERS, rows, 1, dtype=F32),
        shape(rows, width, dtype=F32), shape(head_rows, columns, dtype=F32),
        shape(head_rows, columns, dtype=F32),
    ]
    (input_grad, small, q_grad, o_grad, i_grad, d_grad, q_gain, i_gain, g_first, g_out,
     g_skip) = pl.pallas_call(
        lambda *refs: backward_kernel(levels, *refs),
        out_shape=outs,
        in_specs=[VMEM] * 6 + [ANY] * 19,
        out_specs=[VMEM, VMEM, ANY, VMEM, ANY] + [VMEM] * (len(outs) - 5),
        scratch_shapes=exchange_scratch(width, PHASES)
        + [pltpu.VMEM((2,) + in_blocks + (width,), BF)]
        + [pltpu.VMEM(dims, F32 if dims[0] == LAYERS and dims[1] == BLOCK else BF) for dims in kept_shapes]
        + [pltpu.VMEM((tokens, q_cols), BF)]
        + [pltpu.VMEM((stage_rows[m], cols[m]), BF) for m in range(7)]
        + [
            pltpu.VMEM((LAYERS if m < 4 else 1, levels, chunk[m], cols[m]), BF)
            for m in range(7)
        ]
        + [
            pltpu.VMEM((LAYERS if m < 4 else 1, chunk[m], cols[m]), BF) for m in (0, 1, 2, 4)
        ]
        + [pltpu.VMEM((chunk[0], max(f_cols, q_cols)), F32), pltpu.VMEM((out_rows, width), F32)]
        + [pltpu.VMEM((LAYERS, out_rows, width), BF)] * 2
        + [
            pltpu.VMEM((2, 8, h_cols), F32), pltpu.VMEM((8, h_cols), F32),
            pltpu.VMEM((levels, 8, small_cols), F32),
            pltpu.VMEM((rows, max(ff, 3 * width)), F32),
            pltpu.SemaphoreType.DMA((2, LAYERS, 7, levels)),
            pltpu.SemaphoreType.DMA((20,)),
            pltpu.SemaphoreType.DMA((2, levels)),
            pltpu.SemaphoreType.DMA((2, LAYERS, 3, PLANE)),
            pltpu.SemaphoreType.DMA((2, LAYERS)),
            pltpu.SemaphoreType.DMA((1,)),
        ],
        compiler_params=pltpu.CompilerParams(
            collective_id=2, has_side_effects=True, vmem_limit_bytes=62 * MIB
        ),
        name="decoder_backward",
    )(rope, sel_q, sel_o, gains, w_qkv, w_in, grad_final, nml, act, gl, wi, wd, mid, nrm, qkv, prb,
      att, wq, wo, xs, lines, gpre, hidden.reshape(in_blocks + (h_cols,)),
      picked.reshape(in_blocks + (h_cols,)), g)

    z, narrow = lax.axis_index("wide") // 4, lax.axis_index("narrow")
    g_first_bias = lax.dynamic_slice(small[0], (columns + z * head_rows + narrow * rows,), (rows,))
    return (
        predictions, input_grad, q_grad, o_grad, i_grad, d_grad[:, :ff_rows], q_gain[..., 0],
        i_gain[..., 0], g_first, g_first_bias, g_out[:head_share], small[0, :columns],
        g_skip[:head_share],
    )


def solution(mesh):
    devices = mesh.shape["wide"] * mesh.shape["narrow"]
    both = ("wide", "narrow")
    weight, gain = P(None, both, None), P(None, both)
    return jax.shard_map(
        lambda *arrays: per_device(devices, *arrays),
        mesh=mesh,
        in_specs=(
            P(both, None), P(both), P(both), weight, weight, weight, weight, gain, gain, P(), P(),
            P(None, "narrow"), P("narrow"), P(None, "narrow"), P("wide", "narrow"),
        ),
        out_specs=(
            P("wide", "narrow"), P(both, None), weight, weight, weight, weight, gain, gain,
            P(both, None), P(both), P("wide", "narrow"), P("narrow"), P("wide", "narrow"),
        ),
        check_vma=False,
    )
```

profile of v0, /device:TPU:13, one launch (start us, length us, event | category | flops | bytes accessed | tf_op | source)
XLA Modules:
  0.0 535.0 jit_solution(7636217543892289172)
XLA Ops:
  0.7 0.7 broadcast_compare_fusion
  1.3 0.1 eq.80
  1.4 0.7 eq.74
  2.2 0.7 pad_maximum_fusion
  2.9 1.3 broadcast_in_dim.5.refs_8_
  4.1 1.3 broadcast_in_dim.4.refs_7_
  5.4 0.1 iota_compare_fusion
  5.5 0.1 or_and_fusion
  5.6 0.7 fusion.refs_1_
  6.3 0.1 copy.36
  6.4 0.6 convert_element_type.14.refs_9_.refs_3_
  7.1 267.4 %decoder_forward.1 = (bf16[256,640]{1,0:T(8,128)(2,1)}, f32[128,1280]{1,0:T(8,128)}, f32[2,128,1280]{2,1,0:T(8,128)}, f32[2,128,1280]{2,1,0:T(8,128)}, bf16[2,2,...) custom-call(bf16[128,1280]{1,0:T(8,128)(2,1)} %refs_0_.2, ...), custom_call_target="tpu_custom_call" | custom-call | tf_op jit(solution)/shard_map/decoder_forward/pallas_call | solution.py:1276
  274.5 0.0 copy-start.4
  274.5 244.8 %decoder_backward.1 = (f32[128,1280]{1,0:T(8,128)}, f32[8,1024]{1,0:T(8,128)}, f32[2,40,3840]{2,1,0:T(8,128)}, f32[2,40,1280]{2,1,0:T(8,128)}, f32[2,40,5120]{2,...) custom-call(f32[256,256]{1,0:T(8,128)} %constant.96.clone.refs_2_.re, ...), custom_call_target="tpu_custom_call" | custom-call | tf_op jit(solution)/shard_map/decoder_backward/pallas_call | solution.py:1333
  519.3 0.0 copy-start.2
  519.3 1.5 reduce
  520.8 1.4 reduce.1
  522.2 1.3 slice_reduce_fusion
  523.6 0.8 slice.6
  524.3 0.6 dynamic-slice_bitcast_fusion
  524.9 0.7 copy.46
  525.6 2.0 copy.47
  527.7 0.0 copy-done.2
  527.7 1.0 copy.48
  528.7 0.8 copy.49
  529.5 0.1 copy-done.1
  529.5 1.2 copy.50
  530.7 0.9 copy-done
  531.6 1.2 copy.51
  532.7 0.7 copy.52
  533.4 0.7 copy.53
  534.1 0.7 copy.54
  (13 shorter events, 0.0 us)
Async XLA Ops:
  274.5 250.4 %copy-start.4 = (bf16[256,640]{1,0:T(8,128)(2,1)S(1)}, bf16[256,640]{1,0:T(8,128)(2,1)}, u32[]{:S(2)}) copy-start(bf16[256,640]{1,0:T(8,128)(2,1)} %get-tuple-element.90) | copy-start | bytes 983044
  519.3 8.4 %copy-start.2 = (f32[2,40,3840]{2,1,0:T(8,128)S(1)}, f32[2,40,3840]{2,1,0:T(8,128)}, u32[]{:S(2)}) copy-start(f32[2,40,3840]{2,1,0:T(8,128)} %get-tuple-element.92) | copy-start | bytes 3686404
  525.6 3.1 copy-start.3
  527.7 1.9 copy-start.1
  529.5 2.0 copy-start
  531.6 1.2 copy-start.7
  531.6 1.9 copy-start.6
  531.6 2.5 copy-start.5
where the time goes:
time: 546 us; the launch traced here: 535 us
  Pallas kernels  512 us (94%)
  local copies, waits for them, and re-layouts  16 us (3%)
  other arithmetic  5.83 us (1%)
    pallas_call x1, Pallas kernels, per_device(): pl.pallas_call(lambda *refs: forward_kernel(levels, *refs), out_shape=out...  267 us
    pallas_call x1, Pallas kernels, per_device(): pl.pallas_call(lambda *refs: backward_kernel(levels, *refs), out_shape=ou...  245 us

commit v1 on v0

--- a/solution.py
+++ b/solution.py
@@ -246,6 +246,10 @@
             def _():
                 self.far_stage(0)
 
+            @pl.when(i == 3)
+            def _():
+                self.near_stage(0)
+
             if not taken:
                 pl.when(half == 1)(lambda: self.from_sibling(s, 2).wait_recv())
 
@@ -255,7 +259,6 @@
             return carry
 
         lax.fori_loop(0, 4, body, 0)
-        self.near_stage(0)
         self.far_stage(1)
 
 

time: 546 us -> 547 us (level)
  no operation moved by 1% of the time
where the time goes in v1:
time: 547 us; the launch traced here: 536 us
  Pallas kernels  513 us (94%)
  local copies, waits for them, and re-layouts  16 us (3%)
  other arithmetic  5.83 us (1%)
    pallas_call x1, Pallas kernels, per_device(): pl.pallas_call(lambda *refs: forward_kernel(levels, *refs), out_shape=out...  271 us
    pallas_call x1, Pallas kernels, per_device(): pl.pallas_call(lambda *refs: backward_kernel(levels, *refs), out_shape=ou...  242 us

profile of v1, /device:TPU:13, one launch (start us, length us, event | category | flops | bytes accessed | tf_op | source)
XLA Modules:
  0.0 536.3 jit_solution(9435255834050485227)
XLA Ops:
  0.7 0.7 broadcast_compare_fusion
  1.3 0.1 eq.80
  1.4 0.7 eq.74
  2.2 0.7 pad_maximum_fusion
  2.9 1.3 broadcast_in_dim.5.refs_8_
  4.1 1.3 broadcast_in_dim.4.refs_7_
  5.4 0.1 iota_compare_fusion
  5.5 0.1 or_and_fusion
  5.6 0.7 fusion.refs_1_
  6.3 0.1 copy.36
  6.4 0.6 convert_element_type.14.refs_9_.refs_3_
  7.1 270.9 %decoder_forward.1 = (bf16[256,640]{1,0:T(8,128)(2,1)}, f32[128,1280]{1,0:T(8,128)}, f32[2,128,1280]{2,1,0:T(8,128)}, f32[2,128,1280]{2,1,0:T(8,128)}, bf16[2,2,...) custom-call(bf16[128,1280]{1,0:T(8,128)(2,1)} %refs_0_.2, ...), custom_call_target="tpu_custom_call" | custom-call | tf_op jit(solution)/shard_map/decoder_forward/pallas_call | solution.py:1279
  278.0 0.0 copy-start.4
  278.0 242.4 %decoder_backward.1 = (f32[128,1280]{1,0:T(8,128)}, f32[8,1024]{1,0:T(8,128)}, f32[2,40,3840]{2,1,0:T(8,128)}, f32[2,40,1280]{2,1,0:T(8,128)}, f32[2,40,5120]{2,...) custom-call(f32[256,256]{1,0:T(8,128)} %constant.96.clone.refs_2_.re, ...), custom_call_target="tpu_custom_call" | custom-call | tf_op jit(solution)/shard_map/decoder_backward/pallas_call | solution.py:1336
  520.4 0.0 copy-start.2
  520.4 1.5 reduce
  521.9 1.4 reduce.1
  523.3 1.3 slice_reduce_fusion
  524.7 0.8 slice.6
  525.4 0.6 dynamic-slice_bitcast_fusion
  526.0 0.0 copy-done.4
  526.0 0.7 copy.46
  526.7 2.0 copy.47
  528.8 1.0 copy.48
  529.8 0.8 copy.49
  530.6 0.1 copy-done.1
  530.6 1.2 copy.50
  531.8 0.9 copy-done
  532.7 1.2 copy.51
  533.8 0.7 copy.52
  534.5 0.7 copy.53
  535.2 0.7 copy.54
  (13 shorter events, 0.0 us)
Async XLA Ops:
  278.0 248.0 %copy-start.4 = (bf16[256,640]{1,0:T(8,128)(2,1)S(1)}, bf16[256,640]{1,0:T(8,128)(2,1)}, u32[]{:S(2)}) copy-start(bf16[256,640]{1,0:T(8,128)(2,1)} %get-tuple-element.90) | copy-start | bytes 983044
  520.4 8.4 %copy-start.2 = (f32[2,40,3840]{2,1,0:T(8,128)S(1)}, f32[2,40,3840]{2,1,0:T(8,128)}, u32[]{:S(2)}) copy-start(f32[2,40,3840]{2,1,0:T(8,128)} %get-tuple-element.92) | copy-start | bytes 3686404
  526.7 3.1 copy-start.3
  528.8 1.9 copy-start.1
  530.6 2.0 copy-start
  532.7 1.2 copy-start.7
  532.7 1.9 copy-start.6
  532.7 2.5 copy-start.5
